TPU v7x, 32 devices: a whole 2x2x4 slice. The times are simulated.
32 devices in a mesh: rep: 2 (over y), seq: 4 (over z), mp: 2 (over x), sub: 2 (over core).
Axes of the slice: x: 2, y: 2, z: 4, core: 2. Of those that a mesh axis runs over, the one named last changes fastest.
Arguments:
- normed_inputs: bfloat16 [4096, 5120], P(('rep', 'seq', 'sub'), 'mp'), parts along dimension 0, may hold values from -6 to 6
- base_queries: bfloat16 [4096, 8192], P(('rep', 'seq', 'sub'), 'mp'), parts along dimension 0, may hold values from -8 to 8
- base_keys: bfloat16 [4096, 1024], P(('rep', 'seq', 'sub'), 'mp'), parts along dimension 0, may hold values from -8 to 8
- base_values: bfloat16 [4096, 1024], P(('rep', 'seq', 'sub'), 'mp'), parts along dimension 0, may hold values from -6 to 6
- adapter_down: bfloat16 [8, 5120, 16], P(None, 'mp'), may hold values from -0.078125 to 0.078125
- adapter_up: bfloat16 [8, 16, 8192], P(None, None, 'mp'), may hold values from -0.75 to 0.75
- position_document: int32 [4096], P(('rep', 'seq', 'sub')), parts along dimension 0, may hold values from 0 to 15, never falling along the last dimension, each value on 1 to 768 neighbouring positions
- document_tenant: int32 [32], P('rep'), parts along dimension 0, may hold values from 0 to 7, as said below
- output_gradient: bfloat16 [4096, 8192], P(('rep', 'seq', 'sub'), 'mp'), parts along dimension 0, may hold values from -6 to 6
Outputs:
- attn_out: bfloat16 [4096, 8192], P(('rep', 'seq', 'sub'), 'mp'), parts along dimension 0
- grad_a: float32 [16, 5120, 16], P('rep', 'mp'), parts along dimension 0
- grad_b: float32 [16, 16, 8192], P('rep', None, 'mp'), parts along dimension 0
There are 2 independent parts, one for each index of `rep`. A program takes and returns all parts, laid end to end along the dimension named above; an argument that names none is the same for every part. Nothing has to cross between parts.
Inputs may be any that keep to these rules, and one draw needn't show every extreme that they name: `position_document`: Non-decreasing along the row; each document spans 1 to 768 positions, and one spans exactly that many. `document_tenant`: every tenant owns exactly 2 documents.
All inputs are finite; a program needn't handle non-finite values.
Results may differ from a plain program's by a relative error of at most 0.035.
Values may be sent and summed in bfloat16 or wider, within the bound.
No kernel may reach another device: no remote copies, remote signals or barrier semaphores. Data moves between devices by JAX's collectives and lax.ppermute only.
A program may use at most 192 MiB of HBM per device.

v0:
```python
import functools

import jax
import jax.numpy as jnp
from jax import lax
from jax.experimental import pallas as pl
from jax.experimental.pallas import tpu as pltpu
from jax.sharding import PartitionSpec as P

HEAD = 128
REACH = 3
NEG = -1e30
LIFT = 2.0
LOG2E = 1.4426950408889634
TAIL = 16
VMEM_BYTES = 48 * 1024 * 1024

VM = pl.BlockSpec(memory_space=pltpu.VMEM)
SM = pl.BlockSpec(memory_space=pltpu.SMEM)
ANY = pl.BlockSpec(memory_space=pl.ANY)


def nt(a, b):
    return lax.dot_general(a, b, (((1,), (1,)), ((), ())), preferred_element_type=jnp.float32)


def nn(a, b):
    return jnp.dot(a, b, preferred_element_type=jnp.float32)


def params():
    return pltpu.CompilerParams(vmem_limit_bytes=VMEM_BYTES)


def pack_kernel(keys, values, doc, *outs):
    rows = keys.shape[0]
    half = outs[0].shape[1] // 2
    ids = jnp.broadcast_to((doc[...] + 1).astype(jnp.float32), (TAIL, rows)).astype(jnp.bfloat16)
    for c, out in enumerate(outs):
        out[0:rows, 0:half] = keys[:, c * half : (c + 1) * half]
        out[0:rows, half:] = values[:, c * half : (c + 1) * half]
        out[rows:, :] = jnp.zeros((TAIL, 2 * half), jnp.bfloat16)
        out[rows:, 0:rows] = ids


def pack(keys, values, doc, chunks):
    rows, width = keys.shape
    shape = jax.ShapeDtypeStruct((rows + TAIL, 2 * width // chunks), jnp.bfloat16)
    return pl.pallas_call(
        pack_kernel,
        out_shape=[shape] * chunks,
        in_specs=[VM] * 3,
        out_specs=[VM] * chunks,
        compiler_params=params(),
        cost_estimate=pl.CostEstimate(flops=0, bytes_accessed=8 * rows * width, transcendentals=0),
        name="pack_keys_values",
    )(keys, values, doc)


def relay_kernel(own, got, out, sem):
    sub = lax.axis_index("sub")

    @pl.when(sub == 0)
    def _():
        copy = pltpu.make_async_copy(own, out, sem)
        copy.start()
        copy.wait()

    @pl.when(sub != 0)
    def _():
        copy = pltpu.make_async_copy(got, out, sem)
        copy.start()
        copy.wait()


def relay(own, got):
    return pl.pallas_call(
        relay_kernel,
        out_shape=jax.ShapeDtypeStruct(own.shape, own.dtype),
        in_specs=[ANY, ANY],
        out_specs=ANY,
        scratch_shapes=[pltpu.SemaphoreType.DMA(())],
        compiler_params=params(),
        cost_estimate=pl.CostEstimate(flops=0, bytes_accessed=4 * own.size, transcendentals=0),
        name="relay_block",
    )(own, got)


def selector_of(owner, tenants, rank):
    rows = owner.shape[1]
    tenant = lax.broadcasted_iota(jnp.int32, (tenants * rank, rows), 0) // rank
    return tenant == owner


def fold(full, owner, tenants, rank):
    kept = jnp.where(selector_of(owner, tenants, rank), full, 0.0)
    total = kept[0:rank]
    for t in range(1, tenants):
        total = total + kept[t * rank : (t + 1) * rank]
    return total


def unfold(compact, owner, tenants, rank):
    spread = jnp.concatenate([compact] * tenants, axis=0)
    return jnp.where(selector_of(owner, tenants, rank), spread, 0.0)


def down_kernel(tenants, rank, x, adapter, doc, tenant_of, compact, owner):
    ids = doc[...]
    found = jnp.zeros(ids.shape, jnp.int32)
    for s in range(tenant_of.shape[0]):
        found = jnp.where(ids == s, tenant_of[s], found)
    owner[...] = found
    compact[...] = fold(nt(x[...], adapter[...]).T, found, tenants, rank)


def down_project(x, adapter, doc, tenant_of, tenants, rank):
    rows, width = x.shape
    return pl.pallas_call(
        functools.partial(down_kernel, tenants, rank),
        out_shape=[
            jax.ShapeDtypeStruct((rank, rows), jnp.float32),
            jax.ShapeDtypeStruct((1, rows), jnp.int32),
        ],
        in_specs=[VM, VM, VM, SM],
        out_specs=[VM, VM],
        compiler_params=params(),
        cost_estimate=pl.CostEstimate(
            flops=2 * rows * width * tenants * rank,
            bytes_accessed=2 * width * (rows + tenants * rank),
            transcendentals=0,
        ),
        name="down_project",
    )(x, adapter, doc, tenant_of)


def attention_kernel(
    tenants, rank, group, first,
    base, grad, up, own_k, own_v, two_k, two_v, swap_k, swap_v, pass_k, pass_v,
    own_c, other_c, owner, own_tail, two_tail, swap_tail, pass_tail, *rest,
):
    if first:
        out, part_b, gdown, *scratch = rest
        gdown_before = None
    else:
        gdown_before, _, out, part_b, gdown, *scratch = rest
    bottle, bottle_t, bias, query, gquery, kt, kw, vt, vw, s_ref, gsum, blocks = scratch
    rows = base.shape[0]
    sub = lax.axis_index("sub")
    step = pl.program_id(0)
    last = pl.num_programs(0) - 1
    scale = HEAD**-0.5

    @pl.when(step == 0)
    def _():
        lifted = unfold(own_c[...] + other_c[...], owner[...], tenants, rank)
        bottle_t[...] = lifted.astype(jnp.bfloat16)
        bottle[...] = lifted.T.astype(jnp.bfloat16)
        gsum[...] = jnp.zeros_like(gsum)
        mine = own_tail[0:1, 0:rows].astype(jnp.float32)
        column = jnp.broadcast_to(mine, (rows, rows)).T
        swapped = swap_tail[0:1, 0:rows].astype(jnp.float32)
        passed = pass_tail[0:1, 0:rows].astype(jnp.float32)
        near = jnp.where(sub == 0, swapped, passed)
        far = jnp.where(sub == 0, passed, swapped)
        two = two_tail[0:1, 0:rows].astype(jnp.float32)
        for d, ids in ((3, far), (2, two), (1, near)):
            at = (REACH - d) * rows
            bias[:, at : at + rows] = jnp.where(column == ids, 0.0, NEG)
        causal = lax.broadcasted_iota(jnp.int32, (rows, rows), 0) >= lax.broadcasted_iota(
            jnp.int32, (rows, rows), 1
        )
        bias[:, REACH * rows :] = jnp.where(causal & (column == mine), 0.0, NEG)
        head = jnp.min(mine)
        reach = jnp.where(jnp.max(near) == head, 1, 0)
        reach = jnp.where(jnp.max(two) == head, 2, reach)
        blocks[0] = jnp.where(jnp.max(far) == head, 3, reach)

    ones = jnp.ones((rows, HEAD), jnp.bfloat16)

    def place(slot, k_block, v_block):
        at = pl.ds(slot * rows, rows)
        k = k_block[0:rows, :]
        v = v_block[0:rows, :]
        kw[at, :] = k
        vw[at, 0:HEAD] = v
        vw[at, HEAD:] = ones
        kt[:, at] = k.T
        vt[:, at] = v.T

    place(REACH, own_k, own_v)
    place(REACH - 2, two_k, two_v)

    @pl.when(sub == 0)
    def _():
        place(REACH - 1, swap_k, swap_v)
        place(REACH - 3, pass_k, pass_v)

    @pl.when(sub != 0)
    def _():
        place(REACH - 1, pass_k, pass_v)
        place(REACH - 3, swap_k, swap_v)

    query[...] = (base[...].astype(jnp.float32) + LIFT * nn(bottle[...], up[...])).astype(
        jnp.bfloat16
    )

    def run(count, heads):
        chunks = range(REACH - count, REACH + 1)
        cols = [pl.ds(h * HEAD, HEAD) for h in heads]
        slots = range(len(heads))

        def keys(c):
            return slice(c * rows, (c + 1) * rows)

        def lanes_max(s):
            m = s[:, 0:HEAD]
            for at in range(HEAD, rows, HEAD):
                m = jnp.maximum(m, s[:, at : at + HEAD])
            return m

        peaks = [None] * len(heads)
        for c in chunks:
            for i in slots:
                s = nn(query[:, cols[i]], kt[:, keys(c)]) + bias[:, keys(c)]
                s_ref[i, :, keys(c)] = s
                m = lanes_max(s)
                peaks[i] = m if peaks[i] is None else jnp.maximum(peaks[i], m)
        peaks = [jnp.max(m, axis=1, keepdims=True) for m in peaks]
        sums = [None] * len(heads)
        for c in chunks:
            for i in slots:
                w = jnp.exp2((s_ref[i, :, keys(c)] - peaks[i]) * (scale * LOG2E))
                s_ref[i, :, keys(c)] = w
                o = nn(w.astype(jnp.bfloat16), vw[keys(c), :])
                sums[i] = o if sums[i] is None else sums[i] + o
        inverses, rowdots = [], []
        for i in slots:
            inverse = 1.0 / sums[i][:, HEAD:]
            attn = (sums[i][:, 0:HEAD] * inverse).astype(jnp.bfloat16)
            out[:, cols[i]] = attn
            product = grad[:, cols[i]].astype(jnp.float32) * attn.astype(jnp.float32)
            rowdots.append(jnp.sum(product, axis=1, keepdims=True))
            inverses.append(inverse)
        moved = [None] * len(heads)
        for c in chunks:
            for i in slots:
                dprob = nn(grad[:, cols[i]], vt[:, keys(c)])
                ds = (s_ref[i, :, keys(c)] * (dprob - rowdots[i])).astype(jnp.bfloat16)
                dq = nn(ds, kw[keys(c), :])
                moved[i] = dq if moved[i] is None else moved[i] + dq
        for i in slots:
            gquery[:, cols[i]] = (moved[i] * (inverses[i] * (LIFT * scale))).astype(jnp.bfloat16)

    pair = s_ref.shape[0]
    for count in range(REACH + 1):

        @pl.when(blocks[0] == count)
        def _():
            @pl.loop(0, group // pair)
            def _(i):
                run(count, [i * pair + k for k in range(pair)])

    part_b[...] = nn(bottle_t[...], gquery[...]).astype(jnp.bfloat16)
    gsum[...] += nt(up[...], gquery[...])

    @pl.when(step == last)
    def _():
        total = fold(gsum[...], owner[...], tenants, rank)
        gdown[...] = total if gdown_before is None else total + gdown_before[...]


def attention(
    chunk, chunks, base, grad, up, own, two, swap, passed, own_c, other_c, owner, before, tenants, rank
):
    rows, width = base.shape
    payload_rows, payload_width = own.shape
    heads = payload_width // (2 * HEAD)
    group = width // HEAD // (heads * chunks)
    span = group * HEAD
    first = before is None
    offset = chunk * heads
    wide = lambda r: pl.BlockSpec((r, span), lambda i: (0, i + offset))
    key_block = pl.BlockSpec((payload_rows, HEAD), lambda i: (0, i))
    value_block = pl.BlockSpec((payload_rows, HEAD), lambda i: (0, i + heads))
    tail = pl.BlockSpec((TAIL, payload_width), lambda i: (rows // TAIL, 0))
    same = lambda a: pl.BlockSpec(a.shape, lambda i: (0, 0))
    operands = [base, grad, up]
    specs = [wide(rows), wide(rows), wide(up.shape[0])]
    for block in (own, two, swap, passed):
        operands += [block, block]
        specs += [key_block, value_block]
    operands += [own_c, other_c, owner, own, two, swap, passed]
    specs += [same(own_c), same(other_c), same(owner), tail, tail, tail, tail]
    aliases = {}
    if not first:
        operands += [before[2], before[0]]
        specs += [same(before[2]), ANY]
        aliases = {len(operands) - 1: 0}
    window = (REACH + 1) * rows
    pair = 2
    return pl.pallas_call(
        functools.partial(attention_kernel, tenants, rank, group, first),
        grid=(heads,),
        out_shape=[
            jax.ShapeDtypeStruct((rows, width), jnp.bfloat16),
            jax.ShapeDtypeStruct((tenants * rank, heads * span), jnp.bfloat16),
            jax.ShapeDtypeStruct((rank, rows), jnp.float32),
        ],
        in_specs=specs,
        out_specs=[
            wide(rows),
            pl.BlockSpec((tenants * rank, span), lambda i: (0, i)),
            pl.BlockSpec((rank, rows), lambda i: (0, 0)),
        ],
        scratch_shapes=[
            pltpu.VMEM((rows, tenants * rank), jnp.bfloat16),
            pltpu.VMEM((tenants * rank, rows), jnp.bfloat16),
            pltpu.VMEM((rows, window), jnp.float32),
            pltpu.VMEM((rows, span), jnp.bfloat16),
            pltpu.VMEM((rows, span), jnp.bfloat16),
            pltpu.VMEM((HEAD, window), jnp.bfloat16),
            pltpu.VMEM((window, HEAD), jnp.bfloat16),
            pltpu.VMEM((HEAD, window), jnp.bfloat16),
            pltpu.VMEM((window, 2 * HEAD), jnp.bfloat16),
            pltpu.VMEM((pair, rows, window), jnp.float32),
            pltpu.VMEM((tenants * rank, rows), jnp.float32),
            pltpu.SMEM((1,), jnp.int32),
        ],
        input_output_aliases=aliases,
        compiler_params=params(),
        cost_estimate=pl.CostEstimate(
            flops=8 * rows * window * span * heads,
            bytes_accessed=6 * rows * span * heads,
            transcendentals=rows * window * group * heads,
        ),
        name="attention",
    )(*operands)


def part_a_kernel(tenants, rank, own, other, owner, x, out):
    g = unfold(own[...] + other[...], owner[...], tenants, rank).astype(jnp.bfloat16)
    out[...] = nn(g, x[...]).astype(jnp.bfloat16)


def grad_a_part(own, other, owner, x, tenants, rank):
    rows, width = x.shape
    return pl.pallas_call(
        functools.partial(part_a_kernel, tenants, rank),
        out_shape=jax.ShapeDtypeStruct((tenants * rank, width), jnp.bfloat16),
        in_specs=[VM] * 4,
        out_specs=VM,
        compiler_params=params(),
        cost_estimate=pl.CostEstimate(
            flops=2 * rows * width * tenants * rank,
            bytes_accessed=2 * width * (rows + tenants * rank),
            transcendentals=0,
        ),
        name="grad_a_part",
    )(own, other, owner, x)


def swap_over(block, axis):
    return lax.ppermute(block, axis, [(0, 1), (1, 0)])


def terms_over(block, axis):
    if lax.axis_size(axis) == 2:
        return block, swap_over(block, axis)
    return lax.psum(block, axis), jnp.zeros_like(block)


def shift_over(block, axis):
    size = lax.axis_size(axis)
    return lax.ppermute(block, axis, [(i, i + 1) for i in range(size - 1)])


def body(
    normed_inputs, base_queries, base_keys, base_values, adapter_down, adapter_up,
    position_document, document_tenant, output_gradient,
):
    rows, width = normed_inputs.shape
    tenants, _, rank = adapter_down.shape
    up_width = adapter_up.shape[2]
    doc = position_document.reshape(1, rows)
    adapter = jnp.transpose(adapter_down, (0, 2, 1)).reshape(tenants * rank, width)
    up = adapter_up.reshape(tenants * rank, up_width)

    chunks = 2 if base_keys.shape[1] % (2 * HEAD) == 0 else 1

    own = pack(base_keys, base_values, doc, chunks)
    two = [shift_over(block, "seq") for block in own]
    compact, owner = down_project(normed_inputs, adapter, doc, document_tenant, tenants, rank)
    compact, other = terms_over(compact, "mp")
    swapped = [swap_over(block, "sub") for block in two]
    passed = [shift_over(relay(o, t), ("seq", "sub")) for o, t in zip(own, two)]

    before, parts = None, []
    for c in range(chunks):
        before = attention(
            c, chunks, base_queries, output_gradient, up, own[c], two[c], swapped[c], passed[c],
            compact, other, owner, before, tenants, rank,
        )
        parts.append(lax.psum(before[1], ("seq", "sub")))
    attn_out, _, gdown = before
    gdown, other = terms_over(gdown, "mp")
    part_a = grad_a_part(gdown, other, owner, normed_inputs, tenants, rank)
    sum_a = lax.psum(part_a, ("seq", "sub")).astype(jnp.float32)
    grad_a = jnp.transpose(sum_a.reshape(tenants, rank, width), (0, 2, 1))
    sum_b = jnp.concatenate(parts, axis=1).astype(jnp.float32)
    return attn_out, grad_a, sum_b.reshape(tenants, rank, up_width)


def solution(mesh):
    split = P(("rep", "seq", "sub"), "mp")
    in_specs = (
        split, split, split, split, P(None, "mp", None), P(None, None, "mp"),
        P(("rep", "seq", "sub")), P("rep"), split,
    )
    out_specs = (split, P("rep", "mp", None), P("rep", None, "mp"))
    return jax.shard_map(body, mesh=mesh, in_specs=in_specs, out_specs=out_specs, check_vma=False)
```

profile of v0, /device:TPU:0, one launch (start us, length us, event | category | flops | bytes accessed | tf_op | source)
XLA Modules:
  0.0 151.7 jit_solution(5054815586812679952)
XLA Ops:
  7.2 0.0 copy-start
  7.2 0.0 all-reduce.3.cloned.1.call-start
  7.2 0.0 copy-start.2
  7.2 1.0 copy-done.2
  8.3 0.0 copy-start.3
  8.3 0.9 copy-done.3
  9.2 0.0 copy-start.4
  9.2 0.7 copy-done.4
  9.9 4.9 %collective-permute-start.4 = (bf16[272,512]{1,0:T(8,128)(2,1)S(1)}, bf16[272,512]{1,0:T(8,128)(2,1)S(1)}, u32[]{:S(2)}, u32[]{:S(2)}) collective-permute-start(bf16[272,512]{1,0:T(8,128)(2,1)S(1)} %get-tuple-element.16.own.own_k.own_v.own_tail), channel_id=1, source_target_pairs={{0,4},{4,8},{8,12},{1,5},{5,9},{9,13},{2,6},{6,10},{10,14},{3,7},{... | collective-permute-start | bytes 835592 | tf_op jit(solution)/shard_map/ppermute | solution.py:375
  14.9 3.5 %collective-permute-start = (bf16[272,512]{1,0:T(8,128)(2,1)S(1)}, bf16[272,512]{1,0:T(8,128)(2,1)S(1)}, u32[]{:S(2)}, u32[]{:S(2)}) collective-permute-start(bf16[272,512]{1,0:T(8,128)(2,1)S(1)} %get-tuple-element.13.own.own_k.own_v.own_tail), channel_id=1, source_target_pairs={{0,4},{4,8},{8,12},{1,5},{5,9},{9,13},{2,6},{6,10},{10,14},{3,7},{... | collective-permute-start | bytes 835592 | tf_op jit(solution)/shard_map/ppermute | solution.py:375
  18.4 3.5 %collective-permute-done.4.got.two_k.two_v.two_tail = bf16[272,512]{1,0:T(8,128)(2,1)S(1)} collective-permute-done((bf16[272,512]{1,0:T(8,128)(2,1)S(1)}, bf16[272,512]{1,0:T(8,128)(2,1)S(1)}, u32[]{:S(2)}, u32[]{:S(2)}) %collective-permute-start.4) | collective-permute-done | bytes 278560 | tf_op jit(solution)/shard_map/ppermute | solution.py:375
  22.0 1.3 collective-permute-start.6
  23.3 3.3 %collective-permute-start.5 = (bf16[272,512]{1,0:T(8,128)(2,1)S(1)}, bf16[272,512]{1,0:T(8,128)(2,1)S(1)}, u32[]{:S(2)}, u32[]{:S(2)}) collective-permute-start(bf16[272,512]{1,0:T(8,128)(2,1)S(1)} %collective-permute-done.4.got.two_k.two_v.two_tail), channel_id=1, source_target_pairs={{0,1},{1,0},{2,3},{3,2},{4,5},{5,4},{6,7},{7,6},{8,9},{9,8},{10,11... | collective-permute-start | bytes 835592 | tf_op jit(solution)/shard_map/ppermute | solution.py:364
  26.6 0.0 copy-done
  26.6 0.0 copy-start.1
  26.6 1.1 copy-done.1
  27.6 0.0 copy-start.5
  27.6 0.7 copy-done.5
  28.3 0.0 copy-start.6
  28.3 0.7 copy-done.6
  29.0 0.0 copy-start.7
  29.0 1.1 down_project.1
  30.1 1.6 %collective-permute-start.3 = (f32[16,256]{1,0:T(8,128)S(1)}, f32[16,256]{1,0:T(8,128)S(1)}, u32[]{:S(2)}, u32[]{:S(2)}) collective-permute-start(f32[16,256]{1,0:T(8,128)S(1)} %get-tuple-element.14.own_c), channel_id=1, source_target_pairs={{0,2},{2,0},{1,3},{3,1},{4,6},{6,4},{5,7},{7,5},{8,10},{10,8},{9,1... | collective-permute-start | bytes 49160 | tf_op jit(solution)/shard_map/ppermute | solution.py:364
  31.6 0.0 collective-permute-done.got.two_k.two_v.two_tail
  31.6 0.1 relay_block.2
  31.7 1.7 %collective-permute-start.2 = (bf16[272,512]{1,0:T(8,128)(2,1)S(1)}, bf16[272,512]{1,0:T(8,128)(2,1)S(1)}, u32[]{:S(2)}, u32[]{:S(2)}) collective-permute-start(bf16[272,512]{1,0:T(8,128)(2,1)S(1)} %relay_block.2), channel_id=1, source_target_pairs={{0,1},{1,4},{4,5},{5,8},{8,9},{9,12},{12,13},{2,3},{3,6},{6,7},{7,... | collective-permute-start | bytes 835592 | tf_op jit(solution)/shard_map/ppermute | solution.py:375
  33.4 2.0 %collective-permute-start.1 = (bf16[272,512]{1,0:T(8,128)(2,1)S(1)}, bf16[272,512]{1,0:T(8,128)(2,1)S(1)}, u32[]{:S(2)}, u32[]{:S(2)}) collective-permute-start(bf16[272,512]{1,0:T(8,128)(2,1)S(1)} %collective-permute-done.got.two_k.two_v.two_tail), channel_id=1, source_target_pairs={{0,1},{1,0},{2,3},{3,2},{4,5},{5,4},{6,7},{7,6},{8,9},{9,8},{10,11... | collective-permute-start | bytes 835592 | tf_op jit(solution)/shard_map/ppermute | solution.py:364
  35.4 0.0 collective-permute-done.3.other_c
  35.4 0.0 collective-permute-done.6.pass_k.pass_v.pass_tail
  35.4 0.0 collective-permute-done.5.swap_k.swap_v.swap_tail
  35.4 0.0 copy-done.7
  35.4 0.0 copy-start.8
  35.4 1.2 copy-done.8
  36.6 0.0 copy-start.9
  36.6 10.0 %attention.2 = (bf16[256,4096]{1,0:T(8,128)(2,1)}, bf16[128,2048]{1,0:T(8,128)(2,1)}, f32[16,256]{1,0:T(8,128)S(1)}) custom-call(bf16[256,4096]{1,0:T(8,128)(2,1)S(1)} %copy-done.7, bf16[256,4096]{1,0:T(8,128)(2,1)} %grad.3, bf16[128,4096]{1,0:T(8,128)(2,1)S(1)} %bitcast.13, bf16[272,512]{1,0:T(8,128)(2,1)S(1)} %get-tuple-element.16.own.own_k.own_v.own_tail, ...), custom_call_target="tpu_custom_call" | custom-call | flops 4294967296 | bytes 3145728 | tf_op jit(solution)/shard_map/attention/pallas_call | solution.py:302
  46.6 0.0 collective-permute-done.2.pass_k.pass_v.pass_tail
  46.6 0.0 collective-permute-done.1.swap_k.swap_v.swap_tail
  46.6 0.0 copy-done.9
  46.6 10.0 %attention.3 = (bf16[256,4096]{1,0:T(8,128)(2,1)}, bf16[128,2048]{1,0:T(8,128)(2,1)}, f32[16,256]{1,0:T(8,128)S(1)}) custom-call(bf16[256,4096]{1,0:T(8,128)(2,1)S(1)} %copy-done.7, bf16[256,4096]{1,0:T(8,128)(2,1)} %grad.3, bf16[128,4096]{1,0:T(8,128)(2,1)S(1)} %bitcast.14, ...), custom_call_target="tpu_custom_call", output_to_operand_aliasing={{0}: (19, {})} | custom-call | flops 4294967296 | bytes 3145728 | tf_op jit(solution)/shard_map/attention/pallas_call | solution.py:302
  56.6 0.5 collective-permute-start.7
  57.1 3.2 %collective-permute-done.7.other = f32[16,256]{1,0:T(8,128)S(1)} collective-permute-done((f32[16,256]{1,0:T(8,128)S(1)}, f32[16,256]{1,0:T(8,128)S(1)}, u32[]{:S(2)}, u32[]{:S(2)}) %collective-permute-start.7) | collective-permute-done | bytes 16416 | tf_op jit(solution)/shard_map/ppermute | solution.py:364
  60.3 1.2 grad_a_part.1
  61.5 0.0 all-reduce.3.cloned.1.call-update
  61.6 79.4 %all-reduce.3.cloned.1.call-done = (bf16[8,2560,16]{1,2,0:T(8,128)(2,1)}, bf16[8,16,2048]{2,1,0:T(8,128)(2,1)}, bf16[8,16,2048]{2,1,0:T(8,128)(2,1)}) async-done(((bf16[8,2560,16]{1,2,0:T(8,128)(2,1)}, bf16[8,16,2048]{2,1,0:T(8,128)(2,1)}, bf16[8,16,2048]{2,1,0:T(8,128)(2,1)}), (bf16[8,2560,16]{1,2,0:T(8,128)(2,1)}, bf16[8,16,2048]{2,1,0:T(8,128)(2,1)}, ...) | async-done | bytes 1703952 | tf_op jit(solution)/shard_map/psum | solution.py:408
  140.9 2.4 %transpose.11 = f32[8,2560,16]{1,2,0:T(8,128)} convert(bf16[8,2560,16]{1,2,0:T(8,128)(2,1)} %get-tuple-element.23) | non-fusion elementwise | flops 327680 | bytes 1966080 | tf_op jit(solution)/shard_map/transpose | solution.py:409
  143.3 0.0 copy-done.10
  143.3 0.0 copy-done.11
  143.3 1.5 %maximum_convert_fusion = f32[8,16,4096]{2,1,0:T(8,128)} fusion(bf16[8,16,2048]{2,1,0:T(8,128)(2,1)S(1)} %copy-done.10, bf16[8,16,2048]{2,1,0:T(8,128)(2,1)S(1)} %copy-done.11), kind=kLoop, calls=%fused_computation | loop fusion | flops 2097152 | bytes 3145728 | tf_op jit(solution)/shard_map/convert_element_type | solution.py:410
  (4 shorter events, 0.1 us)
Async XLA Ops:
  7.2 19.4 %copy-start = (bf16[256,2560]{1,0:T(8,128)(2,1)S(1)}, bf16[256,2560]{1,0:T(8,128)(2,1)}, u32[]{:S(2)}) copy-start(bf16[256,2560]{1,0:T(8,128)(2,1)} %x.3) | copy-start | bytes 3932164
  7.2 133.7 %all-reduce.3.cloned.1.call-start = ((), (), s32[]{:S(2)}) async-start(), calls=%async_computation | async-start | bytes 3407872 | tf_op jit(solution)/shard_map/psum | solution.py:408
  7.2 1.0 copy-start.2
  8.3 0.9 copy-start.3
  9.2 0.7 copy-start.4
  9.9 12.0 %collective-permute-start.4 = (bf16[272,512]{1,0:T(8,128)(2,1)S(1)}, bf16[272,512]{1,0:T(8,128)(2,1)S(1)}, u32[]{:S(2)}, u32[]{:S(2)}) collective-permute-start(bf16[272,512]{1,0:T(8,128)(2,1)S(1)} %get-tuple-element.16.own.own_k.own_v.own_tail), channel_id=1, source_target_pairs={{0,4},{4,8},{8,12},{1,5},{5,9},{9,13},{2,6},{6,10},{10,14},{3,7},{... | collective-permute-start | bytes 835592 | tf_op jit(solution)/shard_map/ppermute | solution.py:375
  14.9 16.8 %collective-permute-start = (bf16[272,512]{1,0:T(8,128)(2,1)S(1)}, bf16[272,512]{1,0:T(8,128)(2,1)S(1)}, u32[]{:S(2)}, u32[]{:S(2)}) collective-permute-start(bf16[272,512]{1,0:T(8,128)(2,1)S(1)} %get-tuple-element.13.own.own_k.own_v.own_tail), channel_id=1, source_target_pairs={{0,4},{4,8},{8,12},{1,5},{5,9},{9,13},{2,6},{6,10},{10,14},{3,7},{... | collective-permute-start | bytes 835592 | tf_op jit(solution)/shard_map/ppermute | solution.py:375
  22.0 13.4 %collective-permute-start.6 = (bf16[272,512]{1,0:T(8,128)(2,1)S(1)}, bf16[272,512]{1,0:T(8,128)(2,1)S(1)}, u32[]{:S(2)}, u32[]{:S(2)}) collective-permute-start(bf16[272,512]{1,0:T(8,128)(2,1)S(1)} %relay_block.3), channel_id=1, source_target_pairs={{0,1},{1,4},{4,5},{5,8},{8,9},{9,12},{12,13},{2,3},{3,6},{6,7},{7,... | collective-permute-start | bytes 835592 | tf_op jit(solution)/shard_map/ppermute | solution.py:375
  23.3 12.1 %collective-permute-start.5 = (bf16[272,512]{1,0:T(8,128)(2,1)S(1)}, bf16[272,512]{1,0:T(8,128)(2,1)S(1)}, u32[]{:S(2)}, u32[]{:S(2)}) collective-permute-start(bf16[272,512]{1,0:T(8,128)(2,1)S(1)} %collective-permute-done.4.got.two_k.two_v.two_tail), channel_id=1, source_target_pairs={{0,1},{1,0},{2,3},{3,2},{4,5},{5,4},{6,7},{7,6},{8,9},{9,8},{10,11... | collective-permute-start | bytes 835592 | tf_op jit(solution)/shard_map/ppermute | solution.py:364
  26.6 1.1 copy-start.1
  27.6 0.7 copy-start.5
  28.3 0.7 copy-start.6
  29.0 6.4 %copy-start.7 = (bf16[256,4096]{1,0:T(8,128)(2,1)S(1)}, bf16[256,4096]{1,0:T(8,128)(2,1)}, u32[]{:S(2)}) copy-start(bf16[256,4096]{1,0:T(8,128)(2,1)} %base.3) | copy-start | bytes 6291460
  30.1 5.3 %collective-permute-start.3 = (f32[16,256]{1,0:T(8,128)S(1)}, f32[16,256]{1,0:T(8,128)S(1)}, u32[]{:S(2)}, u32[]{:S(2)}) collective-permute-start(f32[16,256]{1,0:T(8,128)S(1)} %get-tuple-element.14.own_c), channel_id=1, source_target_pairs={{0,2},{2,0},{1,3},{3,1},{4,6},{6,4},{5,7},{7,5},{8,10},{10,8},{9,1... | collective-permute-start | bytes 49160 | tf_op jit(solution)/shard_map/ppermute | solution.py:364
  31.7 14.9 %collective-permute-start.2 = (bf16[272,512]{1,0:T(8,128)(2,1)S(1)}, bf16[272,512]{1,0:T(8,128)(2,1)S(1)}, u32[]{:S(2)}, u32[]{:S(2)}) collective-permute-start(bf16[272,512]{1,0:T(8,128)(2,1)S(1)} %relay_block.2), channel_id=1, source_target_pairs={{0,1},{1,4},{4,5},{5,8},{8,9},{9,12},{12,13},{2,3},{3,6},{6,7},{7,... | collective-permute-start | bytes 835592 | tf_op jit(solution)/shard_map/ppermute | solution.py:375
  33.4 13.2 %collective-permute-start.1 = (bf16[272,512]{1,0:T(8,128)(2,1)S(1)}, bf16[272,512]{1,0:T(8,128)(2,1)S(1)}, u32[]{:S(2)}, u32[]{:S(2)}) collective-permute-start(bf16[272,512]{1,0:T(8,128)(2,1)S(1)} %collective-permute-done.got.two_k.two_v.two_tail), channel_id=1, source_target_pairs={{0,1},{1,0},{2,3},{3,2},{4,5},{5,4},{6,7},{7,6},{8,9},{9,8},{10,11... | collective-permute-start | bytes 835592 | tf_op jit(solution)/shard_map/ppermute | solution.py:364
  35.4 1.2 copy-start.8
  36.6 10.0 %copy-start.9 = (bf16[8,16,4096]{2,1,0:T(8,128)(2,1)S(1)}, bf16[8,16,4096]{2,1,0:T(8,128)(2,1)}, u32[]{:S(2)}) copy-start(bf16[8,16,4096]{2,1,0:T(8,128)(2,1)} %param.14) | copy-start | bytes 3145732
  56.6 3.7 %collective-permute-start.7 = (f32[16,256]{1,0:T(8,128)S(1)}, f32[16,256]{1,0:T(8,128)S(1)}, u32[]{:S(2)}, u32[]{:S(2)}) collective-permute-start(f32[16,256]{1,0:T(8,128)S(1)} %get-tuple-element.20.own), channel_id=1, source_target_pairs={{0,2},{2,0},{1,3},{3,1},{4,6},{6,4},{5,7},{7,5},{8,10},{10,8},{9,1... | collective-permute-start | bytes 49160 | tf_op jit(solution)/shard_map/ppermute | solution.py:364
  140.9 2.4 %copy-start.10 = (bf16[8,16,2048]{2,1,0:T(8,128)(2,1)S(1)}, bf16[8,16,2048]{2,1,0:T(8,128)(2,1)}, u32[]{:S(2)}) copy-start(bf16[8,16,2048]{2,1,0:T(8,128)(2,1)} %get-tuple-element.24) | copy-start | bytes 1572868
  140.9 2.4 %copy-start.11 = (bf16[8,16,2048]{2,1,0:T(8,128)(2,1)S(1)}, bf16[8,16,2048]{2,1,0:T(8,128)(2,1)}, u32[]{:S(2)}) copy-start(bf16[8,16,2048]{2,1,0:T(8,128)(2,1)} %get-tuple-element.25) | copy-start | bytes 1572868
Sparse Core Ops, SparseCore 0:
  61.7 79.1 all-reduce.2
where the time goes:
time: 152 us
  waiting for transfers between devices  86.1 us (57%)
  Pallas kernels  22.4 us (15%)
  starting transfers between devices  18.8 us (12%)
  between operations  14.1 us (9%)
  local copies, waits for them, and re-layouts  6.32 us (4%)
  other arithmetic  3.89 us (3%)
    psum x1, waiting for transfers between devices, body(): sum_a = lax.psum(part_a, ('seq', 'sub')).astype(jnp.float32)  79.4 us
    pallas_call x2, Pallas kernels, attention(): pl.pallas_call(functools.partial(attention_kernel, tenants, rank, group,...  20 us
    ppermute x4, starting transfers between devices, shift_over(): return lax.ppermute(block, axis, [(i, i + 1) for i in range(size - 1)])  11.4 us
    ppermute x4, starting transfers between devices, swap_over(): return lax.ppermute(block, axis, [(0, 1), (1, 0)])  7.34 us
    unnamed x24, local copies, waits for them, and re-layouts  6.32 us
    ppermute x4, waiting for transfers between devices, shift_over(): return lax.ppermute(block, axis, [(i, i + 1) for i in range(size - 1)])  3.54 us
    ppermute x4, waiting for transfers between devices, swap_over(): return lax.ppermute(block, axis, [(0, 1), (1, 0)])  3.23 us
  transfers between devices with their start and end apart: 9, of which 3 were waited for; matrix products, arithmetic and copies ran while one was open for 0% of the time, Pallas kernels for 7%

commit v1 on v0

--- a/solution.py
+++ b/solution.py
@@ -14,6 +14,7 @@
 LOG2E = 1.4426950408889634
 TAIL = 16
 VMEM_BYTES = 48 * 1024 * 1024
+VMEM_MOST = 60 * 1024 * 1024
 
 VM = pl.BlockSpec(memory_space=pltpu.VMEM)
 SM = pl.BlockSpec(memory_space=pltpu.SMEM)
@@ -28,19 +29,37 @@
     return jnp.dot(a, b, preferred_element_type=jnp.float32)
 
 
-def params():
-    return pltpu.CompilerParams(vmem_limit_bytes=VMEM_BYTES)
-
-
-def pack_kernel(keys, values, doc, *outs):
+def params(limit=VMEM_BYTES):
+    return pltpu.CompilerParams(vmem_limit_bytes=limit)
+
+
+def fetch(pairs, sems):
+    copies = [pltpu.make_async_copy(src, dst, sems.at[i]) for i, (src, dst) in enumerate(pairs)]
+    for copy in copies:
+        copy.start()
+    return copies
+
+
+def pack_kernel(keys, values, doc, *rest):
+    outs, ids, tail, sems = rest[:-3], rest[-3], rest[-2], rest[-1]
     rows = keys.shape[0]
     half = outs[0].shape[1] // 2
-    ids = jnp.broadcast_to((doc[...] + 1).astype(jnp.float32), (TAIL, rows)).astype(jnp.bfloat16)
+    pairs = [(doc, ids)]
     for c, out in enumerate(outs):
-        out[0:rows, 0:half] = keys[:, c * half : (c + 1) * half]
-        out[0:rows, half:] = values[:, c * half : (c + 1) * half]
-        out[rows:, :] = jnp.zeros((TAIL, 2 * half), jnp.bfloat16)
-        out[rows:, 0:rows] = ids
+        cols = pl.ds(c * half, half)
+        pairs.append((keys.at[:, cols], out.at[pl.ds(0, rows), pl.ds(0, half)]))
+        pairs.append((values.at[:, cols], out.at[pl.ds(0, rows), pl.ds(half, half)]))
+    copies = fetch(pairs, sems)
+    copies[0].wait()
+    tail[...] = jnp.zeros_like(tail)
+    tail[:, 0:rows] = jnp.broadcast_to((ids[...] + 1).astype(jnp.float32), (TAIL, rows)).astype(
+        jnp.bfloat16
+    )
+    copies += fetch(
+        [(tail, out.at[pl.ds(rows, TAIL), :]) for out in outs], sems.at[pl.ds(len(pairs), len(outs))]
+    )
+    for copy in copies[1:]:
+        copy.wait()
 
 
 def pack(keys, values, doc, chunks):
@@ -49,15 +68,20 @@
     return pl.pallas_call(
         pack_kernel,
         out_shape=[shape] * chunks,
-        in_specs=[VM] * 3,
-        out_specs=[VM] * chunks,
-        compiler_params=params(),
+        in_specs=[ANY] * 3,
+        out_specs=[ANY] * chunks,
+        scratch_shapes=[
+            pltpu.VMEM((1, rows), jnp.int32),
+            pltpu.VMEM((TAIL, 2 * width // chunks), jnp.bfloat16),
+            pltpu.SemaphoreType.DMA((1 + 3 * chunks,)),
+        ],
+        compiler_params=params(VMEM_MOST),
         cost_estimate=pl.CostEstimate(flops=0, bytes_accessed=8 * rows * width, transcendentals=0),
         name="pack_keys_values",
     )(keys, values, doc)
 
 
-def relay_kernel(own, got, out, sem):
+def relay_kernel(own, got, after, out, sem):
     sub = lax.axis_index("sub")
 
     @pl.when(sub == 0)
@@ -73,17 +97,17 @@
         copy.wait()
 
 
-def relay(own, got):
+def relay(own, got, after):
     return pl.pallas_call(
         relay_kernel,
         out_shape=jax.ShapeDtypeStruct(own.shape, own.dtype),
-        in_specs=[ANY, ANY],
+        in_specs=[ANY, ANY, ANY],
         out_specs=ANY,
         scratch_shapes=[pltpu.SemaphoreType.DMA(())],
         compiler_params=params(),
         cost_estimate=pl.CostEstimate(flops=0, bytes_accessed=4 * own.size, transcendentals=0),
         name="relay_block",
-    )(own, got)
+    )(own, got, after)
 
 
 def selector_of(owner, tenants, rank):
@@ -105,12 +129,18 @@
     return jnp.where(selector_of(owner, tenants, rank), spread, 0.0)
 
 
-def down_kernel(tenants, rank, x, adapter, doc, tenant_of, compact, owner):
+def down_kernel(
+    tenants, rank, x_hbm, adapter_hbm, doc_hbm, tenant_of, compact, owner, x, adapter, doc, sems
+):
+    copies = fetch([(doc_hbm, doc), (x_hbm, x), (adapter_hbm, adapter)], sems)
+    copies[0].wait()
     ids = doc[...]
     found = jnp.zeros(ids.shape, jnp.int32)
     for s in range(tenant_of.shape[0]):
         found = jnp.where(ids == s, tenant_of[s], found)
     owner[...] = found
+    copies[1].wait()
+    copies[2].wait()
     compact[...] = fold(nt(x[...], adapter[...]).T, found, tenants, rank)
 
 
@@ -122,9 +152,15 @@
             jax.ShapeDtypeStruct((rank, rows), jnp.float32),
             jax.ShapeDtypeStruct((1, rows), jnp.int32),
         ],
-        in_specs=[VM, VM, VM, SM],
+        in_specs=[ANY, ANY, ANY, SM],
         out_specs=[VM, VM],
-        compiler_params=params(),
+        scratch_shapes=[
+            pltpu.VMEM(x.shape, x.dtype),
+            pltpu.VMEM(adapter.shape, adapter.dtype),
+            pltpu.VMEM(doc.shape, doc.dtype),
+            pltpu.SemaphoreType.DMA((3,)),
+        ],
+        compiler_params=params(VMEM_MOST),
         cost_estimate=pl.CostEstimate(
             flops=2 * rows * width * tenants * rank,
             bytes_accessed=2 * width * (rows + tenants * rank),
@@ -177,6 +213,7 @@
         blocks[0] = jnp.where(jnp.max(far) == head, 3, reach)
 
     ones = jnp.ones((rows, HEAD), jnp.bfloat16)
+    ones_two = jnp.ones((2 * HEAD, HEAD), jnp.bfloat16)
 
     def place(slot, k_block, v_block):
         at = pl.ds(slot * rows, rows)
@@ -240,7 +277,10 @@
             attn = (sums[i][:, 0:HEAD] * inverse).astype(jnp.bfloat16)
             out[:, cols[i]] = attn
             product = grad[:, cols[i]].astype(jnp.float32) * attn.astype(jnp.float32)
-            rowdots.append(jnp.sum(product, axis=1, keepdims=True))
+            high = product.astype(jnp.bfloat16)
+            low = (product - high.astype(jnp.float32)).astype(jnp.bfloat16)
+            dot = nn(jnp.concatenate([high, low], axis=1), ones_two)
+            rowdots.append(jnp.concatenate([dot] * (rows // HEAD), axis=1))
             inverses.append(inverse)
         moved = [None] * len(heads)
         for c in chunks:
@@ -298,7 +338,7 @@
         specs += [same(before[2]), ANY]
         aliases = {len(operands) - 1: 0}
     window = (REACH + 1) * rows
-    pair = 2
+    pair = min(4, group)
     return pl.pallas_call(
         functools.partial(attention_kernel, tenants, rank, group, first),
         grid=(heads,),
@@ -360,6 +400,101 @@
     )(own, other, owner, x)
 
 
+def small_call(kernel, name, shapes, *operands, scratch=()):
+    size = sum(2 * a.size for a in operands)
+    return pl.pallas_call(
+        kernel,
+        out_shape=shapes,
+        in_specs=[VM] * len(operands),
+        out_specs=jax.tree.map(lambda _: VM, shapes),
+        scratch_shapes=list(scratch),
+        compiler_params=params(),
+        cost_estimate=pl.CostEstimate(flops=size, bytes_accessed=2 * size, transcendentals=0),
+        name=name,
+    )(*operands)
+
+
+def split_kernel(tenants, rank, own, other, owner, x, *rest):
+    parts, keep, send = rest[:-2], rest[-2], rest[-1]
+    g = unfold(own[...] + other[...], owner[...], tenants, rank).astype(jnp.bfloat16)
+    a = nn(g, x[...]).astype(jnp.bfloat16)
+    half = keep.shape[0]
+    sub = lax.axis_index("sub")
+
+    def put(mine, theirs):
+        for out, at in ((keep, mine * half), (send, theirs * half)):
+            col = 0
+            for part in parts:
+                out[:, col : col + part.shape[1]] = part[at : at + half, :]
+                col += part.shape[1]
+            out[:, col:] = a[at : at + half, :]
+
+    @pl.when(sub == 0)
+    def _():
+        put(0, 1)
+
+    @pl.when(sub != 0)
+    def _():
+        put(1, 0)
+
+
+def add_kernel(keep, got, out):
+    out[...] = (keep[...].astype(jnp.float32) + got[...].astype(jnp.float32)).astype(jnp.bfloat16)
+
+
+def sum_kernel(size, blocks, out):
+    rows = out.shape[0] // size
+    total = blocks[0:rows, :].astype(jnp.float32)
+    for i in range(1, size):
+        total = total + blocks[i * rows : (i + 1) * rows, :].astype(jnp.float32)
+    total = total.astype(jnp.bfloat16)
+    for i in range(size):
+        out[i * rows : (i + 1) * rows, :] = total
+
+
+def finish_kernel(half_ref, other_ref, grad_b, grad_a):
+    sub = lax.axis_index("sub")
+    half = half_ref.shape[0]
+    wide = grad_b.shape[1]
+
+    def put(ref, at):
+        grad_b[at : at + half, :] = ref[:, 0:wide].astype(jnp.float32)
+        grad_a[at : at + half, :] = ref[:, wide:].astype(jnp.float32)
+
+    @pl.when(sub == 0)
+    def _():
+        put(half_ref, 0)
+        put(other_ref, half)
+
+    @pl.when(sub != 0)
+    def _():
+        put(half_ref, half)
+        put(other_ref, 0)
+
+
+def grads_by_halves(parts, own, other, owner, x, tenants, rank):
+    rows, width = tenants * rank, x.shape[1]
+    size = lax.axis_size("seq")
+    wide = sum(part.shape[1] for part in parts)
+    half = jax.ShapeDtypeStruct((rows // 2, wide + width), jnp.bfloat16)
+    keep, send = small_call(
+        functools.partial(split_kernel, tenants, rank), "split_grads", [half, half],
+        own, other, owner, x, *parts,
+    )
+    mine = small_call(add_kernel, "add_cores", half, keep, swap_over(send, "sub"))
+    blocks = lax.all_to_all(mine, "seq", 0, 0, tiled=True)
+    summed = small_call(functools.partial(sum_kernel, size), "sum_grads", half, blocks)
+    gathered = lax.all_to_all(summed, "seq", 0, 0, tiled=True)
+    return small_call(
+        finish_kernel, "finish_grads",
+        [
+            jax.ShapeDtypeStruct((rows, wide), jnp.float32),
+            jax.ShapeDtypeStruct((rows, width), jnp.float32),
+        ],
+        gathered, swap_over(gathered, "sub"),
+    )
+
+
 def swap_over(block, axis):
     return lax.ppermute(block, axis, [(0, 1), (1, 0)])
 
@@ -391,24 +526,30 @@
     own = pack(base_keys, base_values, doc, chunks)
     two = [shift_over(block, "seq") for block in own]
     compact, owner = down_project(normed_inputs, adapter, doc, document_tenant, tenants, rank)
+    swapped = [swap_over(block, "sub") for block in two]
+    passed = [shift_over(relay(o, t, compact), ("seq", "sub")) for o, t in zip(own, two)]
+
     compact, other = terms_over(compact, "mp")
-    swapped = [swap_over(block, "sub") for block in two]
-    passed = [shift_over(relay(o, t), ("seq", "sub")) for o, t in zip(own, two)]
-
+    by_hand = tenants * rank % (2 * TAIL * lax.axis_size("seq")) == 0
     before, parts = None, []
     for c in range(chunks):
         before = attention(
             c, chunks, base_queries, output_gradient, up, own[c], two[c], swapped[c], passed[c],
             compact, other, owner, before, tenants, rank,
         )
-        parts.append(lax.psum(before[1], ("seq", "sub")))
+        parts.append(before[1])
     attn_out, _, gdown = before
     gdown, other = terms_over(gdown, "mp")
-    part_a = grad_a_part(gdown, other, owner, normed_inputs, tenants, rank)
-    sum_a = lax.psum(part_a, ("seq", "sub")).astype(jnp.float32)
-    grad_a = jnp.transpose(sum_a.reshape(tenants, rank, width), (0, 2, 1))
-    sum_b = jnp.concatenate(parts, axis=1).astype(jnp.float32)
-    return attn_out, grad_a, sum_b.reshape(tenants, rank, up_width)
+    if by_hand:
+        grad_b, grad_a = grads_by_halves(
+            parts, gdown, other, owner, normed_inputs, tenants, rank
+        )
+    else:
+        part_a = grad_a_part(gdown, other, owner, normed_inputs, tenants, rank)
+        grad_a = lax.psum(part_a, ("seq", "sub")).astype(jnp.float32)
+        grad_b = lax.psum(jnp.concatenate(parts, axis=1), ("seq", "sub")).astype(jnp.float32)
+    grad_a = jnp.transpose(grad_a.reshape(tenants, rank, width), (0, 2, 1))
+    return attn_out, grad_a, grad_b.reshape(tenants, rank, up_width)
 
 
 def solution(mesh):

time: 152 us -> 139 us (0.914)
  waiting for transfers between devices: 86.1 us -> 8.09 us
  blocking collectives: 0 us -> 60.7 us
  Pallas kernels: 22.4 us -> 41 us
  between operations: 14.1 us -> 0.78 us
  starting transfers between devices: 18.8 us -> 24.2 us
  other arithmetic: 3.89 us -> 0 us
  local copies, waits for them, and re-layouts: 6.32 us -> 2.99 us
    psum x1 -> x0, waiting for transfers between devices: 79.4 us -> none  [body(): sum_a = lax.psum(part_a, ('seq', 'sub')).astype(jnp.float32)]
    all_to_all x0 -> x2, blocking collectives: none -> 60.7 us  [the longest x1 36.7 us: grads_by_halves(): blocks = lax.all_to_all(mine, 'seq', 0, 0, tiled=True)]
    pallas_call x2 -> x5, Pallas kernels: 1.22 us -> 19.8 us  [the longest x1 17.1 us: pack(): pl.pallas_call(pack_kernel, out_shape=[shape] * chunks, in_specs=[ANY] *...]
    ppermute x4 -> x6, starting transfers between devices: 7.34 us -> 12.7 us  [swap_over(): return lax.ppermute(block, axis, [(0, 1), (1, 0)])]
    ppermute x4 -> x6, waiting for transfers between devices: 3.23 us -> 7.6 us  [swap_over(): return lax.ppermute(block, axis, [(0, 1), (1, 0)])]
    unnamed x24 -> x16, local copies, waits for them, and re-layouts: 6.32 us -> 2.99 us
    ppermute x4, waiting for transfers between devices: 3.54 us -> 0.49 us  [shift_over(): return lax.ppermute(block, axis, [(i, i + 1) for i in range(size - 1)])]
    transpose x1 -> x0, other arithmetic: 2.36 us -> none  [body(): grad_a = jnp.transpose(sum_a.reshape(tenants, rank, width), (0, 2, 1))]
  transfers between devices with their start and end apart: 9 -> 10, of which waited for: 3 -> 4; matrix products, arithmetic and copies ran while one was open for 0% -> 0% of each run, Pallas kernels for 7% -> 9%
where the time goes in v1:
time: 139 us; the launch traced here: 138 us
  blocking collectives  60.7 us (44%)
  Pallas kernels  41 us (29%)
  starting transfers between devices  24.2 us (17%)
  waiting for transfers between devices  8.09 us (6%)
  local copies, waits for them, and re-layouts  2.99 us (2%)
    all_to_all x1, blocking collectives, grads_by_halves(): blocks = lax.all_to_all(mine, 'seq', 0, 0, tiled=True)  36.7 us
    all_to_all x1, blocking collectives, grads_by_halves(): gathered = lax.all_to_all(summed, 'seq', 0, 0, tiled=True)  24 us
    pallas_call x2, Pallas kernels, attention(): pl.pallas_call(functools.partial(attention_kernel, tenants, rank, group,...  17.7 us
    pallas_call x1, Pallas kernels, pack(): pl.pallas_call(pack_kernel, out_shape=[shape] * chunks, in_specs=[ANY] *...  17.1 us
    ppermute x6, starting transfers between devices, swap_over(): return lax.ppermute(block, axis, [(0, 1), (1, 0)])  12.7 us
    ppermute x4, starting transfers between devices, shift_over(): return lax.ppermute(block, axis, [(i, i + 1) for i in range(size - 1)])  11.6 us
    ppermute x6, waiting for transfers between devices, swap_over(): return lax.ppermute(block, axis, [(0, 1), (1, 0)])  7.6 us
    pallas_call x1, Pallas kernels, down_project(): pl.pallas_call(functools.partial(down_kernel, tenants, rank), out_shape=[...  3.36 us
  transfers between devices with their start and end apart: 10, of which 4 were waited for; matrix products, arithmetic and copies ran while one was open for 0% of the time, Pallas kernels for 9%

profile of v1, /device:TPU:0, one launch (start us, length us, event | category | flops | bytes accessed | tf_op | source)
XLA Modules:
  0.0 137.8 jit_solution(4048930579420961561)
XLA Ops:
  0.6 0.0 copy-start.7
  0.6 17.1 %pack_keys_values.1 = (bf16[272,512]{1,0:T(8,128)(2,1)}, bf16[272,512]{1,0:T(8,128)(2,1)}) custom-call(bf16[256,512]{1,0:T(8,128)(2,1)} %keys.1, bf16[256,512]{1,0:T(8,128)(2,1)} %values.1, s32[1,256]{1,0:T(1,128)} %bitcast.21), custom_call_target="tpu_custom_call" | custom-call | bytes 1048576 | tf_op jit(solution)/shard_map/pack_keys_values/pallas_call | solution.py:68
  17.7 0.0 copy-start.2
  17.7 0.0 copy-start.1
  17.7 5.1 %collective-permute-start.4 = (bf16[272,512]{1,0:T(8,128)(2,1)}, bf16[272,512]{1,0:T(8,128)(2,1)S(1)}, u32[]{:S(2)}, u32[]{:S(2)}) collective-permute-start(bf16[272,512]{1,0:T(8,128)(2,1)} %get-tuple-element.20.own.own_k.own_v.own_tail), channel_id=1, source_target_pairs={{0,4},{4,8},{8,12},{1,5},{5,9},{9,13},{2,6},{6,10},{10,14},{3,7},{... | collective-permute-start | bytes 835592 | tf_op jit(solution)/shard_map/ppermute | solution.py:510
  22.8 3.5 %collective-permute-start = (bf16[272,512]{1,0:T(8,128)(2,1)}, bf16[272,512]{1,0:T(8,128)(2,1)S(1)}, u32[]{:S(2)}, u32[]{:S(2)}) collective-permute-start(bf16[272,512]{1,0:T(8,128)(2,1)} %get-tuple-element.17.own.own_k.own_v.own_tail), channel_id=1, source_target_pairs={{0,4},{4,8},{8,12},{1,5},{5,9},{9,13},{2,6},{6,10},{10,14},{3,7},{... | collective-permute-start | bytes 835592 | tf_op jit(solution)/shard_map/ppermute | solution.py:510
  26.3 3.4 %down_project.1 = (f32[16,256]{1,0:T(8,128)}, s32[1,256]{1,0:T(1,128)}) custom-call(bf16[256,2560]{1,0:T(8,128)(2,1)} %x.1, bf16[128,2560]{1,0:T(8,128)(2,1)} %bitcast.20, s32[1,256]{1,0:T(1,128)} %bitcast.22, s32[16]{0:T(128)} %tenant_of.1), custom_call_target="tpu_custom_call" | custom-call | flops 167772160 | bytes 1966080 | tf_op jit(solution)/shard_map/down_project/pallas_call | solution.py:149
  29.7 0.5 collective-permute-done.4.got.two_k.two_v.two_tail
  30.2 0.0 copy-done.2
  30.2 0.0 copy-start.3
  30.2 0.7 copy-done.3
  30.9 1.3 collective-permute-start.6
  32.2 3.2 %collective-permute-start.5 = (bf16[272,512]{1,0:T(8,128)(2,1)S(1)}, bf16[272,512]{1,0:T(8,128)(2,1)S(1)}, u32[]{:S(2)}, u32[]{:S(2)}) collective-permute-start(bf16[272,512]{1,0:T(8,128)(2,1)S(1)} %collective-permute-done.4.got.two_k.two_v.two_tail), channel_id=1, source_target_pairs={{0,1},{1,0},{2,3},{3,2},{4,5},{5,4},{6,7},{7,6},{8,9},{9,8},{10,11... | collective-permute-start | bytes 835592 | tf_op jit(solution)/shard_map/ppermute | solution.py:499
  35.4 1.5 %collective-permute-start.3 = (f32[16,256]{1,0:T(8,128)S(1)}, f32[16,256]{1,0:T(8,128)S(1)}, u32[]{:S(2)}, u32[]{:S(2)}) collective-permute-start(f32[16,256]{1,0:T(8,128)S(1)} %copy-done.3), channel_id=1, source_target_pairs={{0,2},{2,0},{1,3},{3,1},{4,6},{6,4},{5,7},{7,5},{8,10},{10,8},{9,1... | collective-permute-start | bytes 49160 | tf_op jit(solution)/shard_map/ppermute | solution.py:499
  36.9 0.0 collective-permute-done.got.two_k.two_v.two_tail
  36.9 0.0 copy-done.1
  36.9 0.1 relay_block.2
  37.0 1.7 %collective-permute-start.2 = (bf16[272,512]{1,0:T(8,128)(2,1)S(1)}, bf16[272,512]{1,0:T(8,128)(2,1)S(1)}, u32[]{:S(2)}, u32[]{:S(2)}) collective-permute-start(bf16[272,512]{1,0:T(8,128)(2,1)S(1)} %relay_block.2), channel_id=1, source_target_pairs={{0,1},{1,4},{4,5},{5,8},{8,9},{9,12},{12,13},{2,3},{3,6},{6,7},{7,... | collective-permute-start | bytes 835592 | tf_op jit(solution)/shard_map/ppermute | solution.py:510
  38.7 2.0 %collective-permute-start.1 = (bf16[272,512]{1,0:T(8,128)(2,1)S(1)}, bf16[272,512]{1,0:T(8,128)(2,1)S(1)}, u32[]{:S(2)}, u32[]{:S(2)}) collective-permute-start(bf16[272,512]{1,0:T(8,128)(2,1)S(1)} %collective-permute-done.got.two_k.two_v.two_tail), channel_id=1, source_target_pairs={{0,1},{1,0},{2,3},{3,2},{4,5},{5,4},{6,7},{7,6},{8,9},{9,8},{10,11... | collective-permute-start | bytes 835592 | tf_op jit(solution)/shard_map/ppermute | solution.py:499
  40.6 0.0 collective-permute-done.3.other_c
  40.6 0.0 collective-permute-done.6.pass_k.pass_v.pass_tail
  40.6 0.0 collective-permute-done.5.swap_k.swap_v.swap_tail
  40.6 0.0 copy-done.7
  40.7 0.0 copy-start.4
  40.7 0.7 copy-done.4
  41.3 0.0 copy-start.6
  41.3 1.6 %copy-done.6 = bf16[256,4096]{1,0:T(8,128)(2,1)S(1)} copy-done((bf16[256,4096]{1,0:T(8,128)(2,1)S(1)}, bf16[256,4096]{1,0:T(8,128)(2,1)}, u32[]{:S(2)}) %copy-start.6) | copy-done | bytes 2097176
  42.9 8.7 %attention.2 = (bf16[256,4096]{1,0:T(8,128)(2,1)}, bf16[128,2048]{1,0:T(8,128)(2,1)S(1)}, f32[16,256]{1,0:T(8,128)S(1)}) custom-call(bf16[256,4096]{1,0:T(8,128)(2,1)S(1)} %copy-done.6, bf16[256,4096]{1,0:T(8,128)(2,1)} %grad.3, bf16[128,4096]{1,0:T(8,128)(2,1)S(1)} %bitcast.18, bf16[272,512]{1,0:T(8,128)(2,1)S(1)} %copy-done.2, ...), custom_call_target="tpu_custom_call" | custom-call | flops 4294967296 | bytes 3145728 | tf_op jit(solution)/shard_map/attention/pallas_call | solution.py:342
  51.6 0.0 collective-permute-done.2.pass_k.pass_v.pass_tail
  51.6 0.0 collective-permute-done.1.swap_k.swap_v.swap_tail
  51.6 0.0 copy-start
  51.6 0.0 copy-start.5
  51.6 9.0 %attention.3 = (bf16[256,4096]{1,0:T(8,128)(2,1)}, bf16[128,2048]{1,0:T(8,128)(2,1)S(1)}, f32[16,256]{1,0:T(8,128)S(1)}) custom-call(bf16[256,4096]{1,0:T(8,128)(2,1)S(1)} %copy-done.6, bf16[256,4096]{1,0:T(8,128)(2,1)} %grad.3, bf16[128,4096]{1,0:T(8,128)(2,1)S(1)} %bitcast.19, bf16[272,512]{1,0:T(8,128)(2,1)S(1)} %copy-done.1, ...), custom_call_target="tpu_custom_call", output_to_operand_aliasing={{0}: (19, {})} | custom-call | flops 4294967296 | bytes 3145728 | tf_op jit(solution)/shard_map/attention/pallas_call | solution.py:342
  60.6 0.5 collective-permute-start.7
  61.2 3.2 %collective-permute-done.7.other = f32[16,256]{1,0:T(8,128)S(1)} collective-permute-done((f32[16,256]{1,0:T(8,128)S(1)}, f32[16,256]{1,0:T(8,128)S(1)}, u32[]{:S(2)}, u32[]{:S(2)}) %collective-permute-start.7) | collective-permute-done | bytes 16416 | tf_op jit(solution)/shard_map/ppermute | solution.py:499
  64.4 0.0 copy-done
  64.4 0.0 copy-done.5
  64.4 0.5 split_grads.1
  64.9 5.5 %collective-permute-start.8 = (bf16[64,6656]{1,0:T(8,128)(2,1)S(1)}, bf16[64,6656]{1,0:T(8,128)(2,1)S(1)}, u32[]{:S(2)}, u32[]{:S(2)}) collective-permute-start(bf16[64,6656]{1,0:T(8,128)(2,1)S(1)} %get-tuple-element.28), channel_id=1, source_target_pairs={{0,1},{1,0},{2,3},{3,2},{4,5},{5,4},{6,7},{7,6},{8,9},{9,8},{10,11... | collective-permute-start | bytes 2555912 | tf_op jit(solution)/shard_map/ppermute | solution.py:499
  70.4 2.0 %collective-permute-done.8.got = bf16[64,6656]{1,0:T(8,128)(2,1)S(1)} collective-permute-done((bf16[64,6656]{1,0:T(8,128)(2,1)S(1)}, bf16[64,6656]{1,0:T(8,128)(2,1)S(1)}, u32[]{:S(2)}, u32[]{:S(2)}) %collective-permute-start.8) | collective-permute-done | bytes 852000 | tf_op jit(solution)/shard_map/ppermute | solution.py:499
  72.4 0.2 add_cores.1
  72.6 36.7 %all_to_all.22 = bf16[4,16,6656]{2,1,0:T(8,128)(2,1)S(1)} all-to-all(bf16[4,16,6656]{2,1,0:T(8,128)(2,1)S(1)} %bitcast.13), channel_id=1, replica_groups=mesh['rep'=2,'seq'=4,'mp'=2,'sub'=2] {'seq'}, dimensions={0} | all-to-all | bytes 1703936 | tf_op jit(solution)/shard_map/all_to_all | solution.py:485
  109.3 0.1 sum_grads.1
  109.4 24.0 %all_to_all.23 = bf16[4,16,6656]{2,1,0:T(8,128)(2,1)S(1)} all-to-all(bf16[4,16,6656]{2,1,0:T(8,128)(2,1)S(1)} %bitcast.17), channel_id=1, replica_groups=mesh['rep'=2,'seq'=4,'mp'=2,'sub'=2] {'seq'}, dimensions={0} | all-to-all | bytes 1703936 | tf_op jit(solution)/shard_map/all_to_all | solution.py:487
  133.4 0.0 collective-permute-start.9
  133.4 2.4 %collective-permute-done.9.other_ref = bf16[64,6656]{1,0:T(8,128)(2,1)S(1)} collective-permute-done((bf16[64,6656]{1,0:T(8,128)(2,1)S(1)}, bf16[64,6656]{1,0:T(8,128)(2,1)S(1)}, u32[]{:S(2)}, u32[]{:S(2)}) %collective-permute-start.9) | collective-permute-done | bytes 852000 | tf_op jit(solution)/shard_map/ppermute | solution.py:499
  135.8 2.0 %finish_grads.1 = (f32[128,4096]{1,0:T(8,128)}, f32[128,2560]{1,0:T(8,128)}) custom-call(bf16[64,6656]{1,0:T(8,128)(2,1)S(1)} %bitcast.15, bf16[64,6656]{1,0:T(8,128)(2,1)S(1)} %collective-permute-done.9.other_ref), custom_call_target="tpu_custom_call" | custom-call | flops 1703936 | bytes 3407872 | tf_op jit(solution)/shard_map/finish_grads/pallas_call | solution.py:405
  (1 shorter events, 0.0 us)
Async XLA Ops:
  0.6 40.0 %copy-start.7 = (bf16[8,16,4096]{2,1,0:T(8,128)(2,1)S(1)}, bf16[8,16,4096]{2,1,0:T(8,128)(2,1)}, u32[]{:S(2)}) copy-start(bf16[8,16,4096]{2,1,0:T(8,128)(2,1)} %param.14) | copy-start | bytes 3145732
  17.7 12.5 %copy-start.2 = (bf16[272,512]{1,0:T(8,128)(2,1)S(1)}, bf16[272,512]{1,0:T(8,128)(2,1)}, u32[]{:S(2)}) copy-start(bf16[272,512]{1,0:T(8,128)(2,1)} %get-tuple-element.20.own.own_k.own_v.own_tail) | copy-start | bytes 835588
  17.7 19.2 %copy-start.1 = (bf16[272,512]{1,0:T(8,128)(2,1)S(1)}, bf16[272,512]{1,0:T(8,128)(2,1)}, u32[]{:S(2)}) copy-start(bf16[272,512]{1,0:T(8,128)(2,1)} %get-tuple-element.17.own.own_k.own_v.own_tail) | copy-start | bytes 835588
  17.7 12.4 %collective-permute-start.4 = (bf16[272,512]{1,0:T(8,128)(2,1)}, bf16[272,512]{1,0:T(8,128)(2,1)S(1)}, u32[]{:S(2)}, u32[]{:S(2)}) collective-permute-start(bf16[272,512]{1,0:T(8,128)(2,1)} %get-tuple-element.20.own.own_k.own_v.own_tail), channel_id=1, source_target_pairs={{0,4},{4,8},{8,12},{1,5},{5,9},{9,13},{2,6},{6,10},{10,14},{3,7},{... | collective-permute-start | bytes 835592 | tf_op jit(solution)/shard_map/ppermute | solution.py:510
  22.8 14.1 %collective-permute-start = (bf16[272,512]{1,0:T(8,128)(2,1)}, bf16[272,512]{1,0:T(8,128)(2,1)S(1)}, u32[]{:S(2)}, u32[]{:S(2)}) collective-permute-start(bf16[272,512]{1,0:T(8,128)(2,1)} %get-tuple-element.17.own.own_k.own_v.own_tail), channel_id=1, source_target_pairs={{0,4},{4,8},{8,12},{1,5},{5,9},{9,13},{2,6},{6,10},{10,14},{3,7},{... | collective-permute-start | bytes 835592 | tf_op jit(solution)/shard_map/ppermute | solution.py:510
  30.2 0.7 copy-start.3
  30.9 9.7 %collective-permute-start.6 = (bf16[272,512]{1,0:T(8,128)(2,1)S(1)}, bf16[272,512]{1,0:T(8,128)(2,1)S(1)}, u32[]{:S(2)}, u32[]{:S(2)}) collective-permute-start(bf16[272,512]{1,0:T(8,128)(2,1)S(1)} %relay_block.3), channel_id=1, source_target_pairs={{0,1},{1,4},{4,5},{5,8},{8,9},{9,12},{12,13},{2,3},{3,6},{6,7},{7,... | collective-permute-start | bytes 835592 | tf_op jit(solution)/shard_map/ppermute | solution.py:510
  32.2 8.4 %collective-permute-start.5 = (bf16[272,512]{1,0:T(8,128)(2,1)S(1)}, bf16[272,512]{1,0:T(8,128)(2,1)S(1)}, u32[]{:S(2)}, u32[]{:S(2)}) collective-permute-start(bf16[272,512]{1,0:T(8,128)(2,1)S(1)} %collective-permute-done.4.got.two_k.two_v.two_tail), channel_id=1, source_target_pairs={{0,1},{1,0},{2,3},{3,2},{4,5},{5,4},{6,7},{7,6},{8,9},{9,8},{10,11... | collective-permute-start | bytes 835592 | tf_op jit(solution)/shard_map/ppermute | solution.py:499
  35.4 5.2 %collective-permute-start.3 = (f32[16,256]{1,0:T(8,128)S(1)}, f32[16,256]{1,0:T(8,128)S(1)}, u32[]{:S(2)}, u32[]{:S(2)}) collective-permute-start(f32[16,256]{1,0:T(8,128)S(1)} %copy-done.3), channel_id=1, source_target_pairs={{0,2},{2,0},{1,3},{3,1},{4,6},{6,4},{5,7},{7,5},{8,10},{10,8},{9,1... | collective-permute-start | bytes 49160 | tf_op jit(solution)/shard_map/ppermute | solution.py:499
  37.0 14.6 %collective-permute-start.2 = (bf16[272,512]{1,0:T(8,128)(2,1)S(1)}, bf16[272,512]{1,0:T(8,128)(2,1)S(1)}, u32[]{:S(2)}, u32[]{:S(2)}) collective-permute-start(bf16[272,512]{1,0:T(8,128)(2,1)S(1)} %relay_block.2), channel_id=1, source_target_pairs={{0,1},{1,4},{4,5},{5,8},{8,9},{9,12},{12,13},{2,3},{3,6},{6,7},{7,... | collective-permute-start | bytes 835592 | tf_op jit(solution)/shard_map/ppermute | solution.py:510
  38.7 12.9 %collective-permute-start.1 = (bf16[272,512]{1,0:T(8,128)(2,1)S(1)}, bf16[272,512]{1,0:T(8,128)(2,1)S(1)}, u32[]{:S(2)}, u32[]{:S(2)}) collective-permute-start(bf16[272,512]{1,0:T(8,128)(2,1)S(1)} %collective-permute-done.got.two_k.two_v.two_tail), channel_id=1, source_target_pairs={{0,1},{1,0},{2,3},{3,2},{4,5},{5,4},{6,7},{7,6},{8,9},{9,8},{10,11... | collective-permute-start | bytes 835592 | tf_op jit(solution)/shard_map/ppermute | solution.py:499
  40.7 0.7 copy-start.4
  41.3 1.6 %copy-start.6 = (bf16[256,4096]{1,0:T(8,128)(2,1)S(1)}, bf16[256,4096]{1,0:T(8,128)(2,1)}, u32[]{:S(2)}) copy-start(bf16[256,4096]{1,0:T(8,128)(2,1)} %base.3) | copy-start | bytes 6291460
  51.6 12.8 %copy-start = (bf16[256,2560]{1,0:T(8,128)(2,1)S(1)}, bf16[256,2560]{1,0:T(8,128)(2,1)}, u32[]{:S(2)}) copy-start(bf16[256,2560]{1,0:T(8,128)(2,1)} %x.1) | copy-start | bytes 3932164
  51.6 12.8 %copy-start.5 = (s32[1,256]{1,0:T(1,128)S(1)}, s32[1,256]{1,0:T(1,128)}, u32[]{:S(2)}) copy-start(s32[1,256]{1,0:T(1,128)} %get-tuple-element.19.owner) | copy-start | bytes 3076
  60.6 3.7 %collective-permute-start.7 = (f32[16,256]{1,0:T(8,128)S(1)}, f32[16,256]{1,0:T(8,128)S(1)}, u32[]{:S(2)}, u32[]{:S(2)}) collective-permute-start(f32[16,256]{1,0:T(8,128)S(1)} %get-tuple-element.24.own), channel_id=1, source_target_pairs={{0,2},{2,0},{1,3},{3,1},{4,6},{6,4},{5,7},{7,5},{8,10},{10,8},{9,1... | collective-permute-start | bytes 49160 | tf_op jit(solution)/shard_map/ppermute | solution.py:499
  64.9 7.5 %collective-permute-start.8 = (bf16[64,6656]{1,0:T(8,128)(2,1)S(1)}, bf16[64,6656]{1,0:T(8,128)(2,1)S(1)}, u32[]{:S(2)}, u32[]{:S(2)}) collective-permute-start(bf16[64,6656]{1,0:T(8,128)(2,1)S(1)} %get-tuple-element.28), channel_id=1, source_target_pairs={{0,1},{1,0},{2,3},{3,2},{4,5},{5,4},{6,7},{7,6},{8,9},{9,8},{10,11... | collective-permute-start | bytes 2555912 | tf_op jit(solution)/shard_map/ppermute | solution.py:499
  133.4 2.4 %collective-permute-start.9 = (bf16[64,6656]{1,0:T(8,128)(2,1)S(1)}, bf16[64,6656]{1,0:T(8,128)(2,1)S(1)}, u32[]{:S(2)}, u32[]{:S(2)}) collective-permute-start(bf16[64,6656]{1,0:T(8,128)(2,1)S(1)} %bitcast.14), channel_id=1, source_target_pairs={{0,1},{1,0},{2,3},{3,2},{4,5},{5,4},{6,7},{7,6},{8,9},{9,8},{10,11... | collective-permute-start | bytes 2555912 | tf_op jit(solution)/shard_map/ppermute | solution.py:499
